TPU v7x, 512 devices: a whole 4x8x8 slice. The times are simulated.
512 devices in a mesh: island: 16 (over x, z_lo), fsdp: 32 (over z_hi, y, core).
Axes of the slice: x: 4, y: 8, z: 8 (z_hi: 2, z_lo: 4; z = z_hi * 4 + z_lo), core: 2. Of those that a mesh axis runs over, the one named last changes fastest.
Arguments:
- key_grad: bfloat16 [65536, 512], P(('island', 'fsdp')), may hold values from -0.25 to 0.25
- layer_input: bfloat16 [65536, 8192], P(('island', 'fsdp')), may hold values from -24 to 24
- key_weight: bfloat16 [16, 8192, 512], P('island', 'fsdp'), may hold values from -0.0625 to 0.0625
- outer_frag: float32 [128, 8192], P(None, 'fsdp'), may hold values from -6 to 6
- momentum: float32 [128, 8192], P(None, 'fsdp'), may hold values from -6 to 6
- inner_frag: bfloat16 [2048, 8192], P('island', 'fsdp'), may hold values from -6 to 6
Outputs:
- keys: bfloat16 [65536, 512], P(('island', 'fsdp'))
- weight_grad: float32 [16, 8192, 512], P('island', 'fsdp')
- new_outer: float32 [128, 8192], P(None, 'fsdp')
- new_momentum: float32 [128, 8192], P(None, 'fsdp')
All inputs are finite; a program needn't handle non-finite values.
Results may differ from a plain program's by a relative error of at most 0.0065.
Values may be sent and summed in bfloat16 or wider, within the bound.
A program may use at most 64 MiB of HBM per device.

v0:
```python
import jax
import jax.numpy as jnp
from jax import lax
from jax.sharding import PartitionSpec as P


def body(key_grad, layer_input, key_weight, outer_frag, momentum, inner_frag):
    weight = key_weight[0]
    tok_rows = key_grad.shape[0]
    features = key_grad.shape[1]
    keys = jnp.dot(
        layer_input,
        lax.all_gather(weight, "fsdp", axis=0, tiled=True),
        preferred_element_type=jnp.float32,
    ).astype(jnp.bfloat16)
    regrouped = lax.all_to_all(layer_input, "fsdp", split_axis=1, concat_axis=0, tiled=True)
    own_rows = regrouped.shape[1]
    width_fsdp = lax.axis_size("fsdp")
    gathered = lax.all_gather(key_grad, "fsdp", axis=0, tiled=True)
    blocks = jnp.einsum(
        "ktd,kte->kde",
        regrouped.reshape(width_fsdp, tok_rows, own_rows),
        gathered.reshape(width_fsdp, tok_rows, features),
        preferred_element_type=jnp.float32,
    )
    grad = jnp.sum(blocks.astype(jnp.bfloat16), axis=0, dtype=jnp.float32)
    delta = outer_frag - inner_frag.astype(jnp.float32)
    width_island = lax.axis_size("island")
    pseudo = lax.psum(delta, "island") / width_island
    new_momentum = 0.9 * momentum + pseudo
    new_outer = outer_frag - 0.7 * (pseudo + 0.9 * new_momentum)
    return (keys, grad[None], new_outer, new_momentum)


def solution(mesh):
    placed = (
        P(("island", "fsdp"), None),
        P(("island", "fsdp"), None),
        P("island", "fsdp", None),
        P(None, "fsdp"),
        P(None, "fsdp"),
        P("island", "fsdp"),
    )
    return jax.shard_map(
        body,
        mesh=mesh,
        in_specs=placed,
        out_specs=(
            P(("island", "fsdp"), None),
            P("island", "fsdp", None),
            P(None, "fsdp"),
            P(None, "fsdp"),
        ),
        check_vma=False,
    )
```

profile of v0, /device:TPU:1, one launch (start us, length us, event | category | flops | bytes accessed | tf_op | source)
XLA Modules:
  0.0 311.8 jit_solution(5166028739397559771)
XLA Ops:
  8.0 0.0 all-reduce.2.cloned.1.call-start
  8.0 1.6 convert_subtract_fusion
  9.6 0.0 all-reduce.2.cloned.1.call-update
  9.6 0.0 all-gather.4.cloned.1.call-start
  9.7 0.5 all-gather.4.cloned.1.call-update
  10.2 0.0 all-gather.6.cloned.1.call-start
  10.3 0.5 all-gather.6.cloned.1.call-update
  10.8 0.0 copy-start.2
  10.8 0.0 copy-start.3
  10.8 4.1 %copy.10 = bf16[128,8192]{0,1:T(8,128)(2,1)} copy(bf16[128,8192]{1,0:T(8,128)(2,1)} %param.7) | data formatting | bytes 4194304 | tf_op args[1]
  15.0 17.2 %all-to-all-start = ((bf16[128,32,256]{0,2,1:T(8,128)(2,1)}), bf16[128,32,256]{0,2,1:T(8,128)(2,1)S(1)}, u32[]{:S(2)}, u32[]{:S(2)}) async-start(bf16[128,32,256]{0,2,1:T(8,128)(2,1)} %bitcast.1), calls=%async_computation | async-start | bytes 4194304 | tf_op jit(solution)/shard_map/all_to_all | solution.py:16
  32.2 248.8 %all-reduce.2.cloned.1.call-done = f32[128,256]{1,0:T(8,128)} async-done(((f32[128,256]{1,0:T(8,128)}), f32[128,256]{1,0:T(8,128)}) %all-reduce.2.cloned.1.call-update) | async-done | bytes 131088 | tf_op jit(solution)/shard_map/psum | solution.py:29
  280.9 0.0 copy-done.2
  280.9 0.0 copy-done.3
  280.9 1.6 multiply_subtract_fusion
  282.6 0.0 all-to-all-done
  282.6 0.0 copy-start.1
  282.6 0.0 all-gather.4.cloned.1.call-done
  282.6 1.3 copy-done.1
  283.9 0.0 copy-start
  283.9 6.2 %convert_reduce_fusion = f32[256,512]{1,0:T(8,128)} fusion(bf16[32,128,512]{2,1,0:T(8,128)(2,1)} %bitcast.13, bf16[128,32,256]{0,2,1:T(8,128)(2,1)} %copy-done.1), kind=kOutput, calls=%fused_computation | convolution fusion | flops 1086193664 | bytes 6815744 | tf_op jit(solution)/shard_map/ktd,kte->kde/dot_general | solution.py:20
  290.1 9.0 %all-gather.6.cloned.1.call-done = bf16[1,8192,512]{2,1,0:T(8,128)(2,1)} async-done(((bf16[1,256,512]{2,1,0:T(8,128)(2,1)}), bf16[1,8192,512]{2,1,0:T(8,128)(2,1)}) %all-gather.6.cloned.1.call-update) | async-done | bytes 8388624 | tf_op jit(solution)/shard_map/all_gather | solution.py:13
  299.1 0.0 copy-done
  299.1 5.3 %fusion.3 = bf16[128,512]{1,0:T(8,128)(2,1)} fusion(bf16[128,8192]{1,0:T(8,128)(2,1)S(1)} %copy-done, bf16[1,8192,512]{2,1,0:T(8,128)(2,1)} %all-gather.6.cloned.1.call-done), kind=kOutput, calls=%fused_computation.4 | convolution fusion | flops 1073807360 | bytes 10616832 | tf_op jit(solution)/shard_map/dot_general | solution.py:11
Async XLA Ops:
  8.0 272.9 %all-reduce.2.cloned.1.call-start = ((), (), s32[]{:S(2)}) async-start(), calls=%async_computation.2 | async-start | bytes 262144 | tf_op jit(solution)/shard_map/psum | solution.py:29
  9.6 272.9 %all-gather.4.cloned.1.call-start = ((), (), s32[]{:S(2)}) async-start(), calls=%async_computation.1 | async-start | bytes 4325376 | tf_op jit(solution)/shard_map/all_gather | solution.py:19
  10.2 288.8 %all-gather.6.cloned.1.call-start = ((), (), s32[]{:S(2)}) async-start(), calls=%async_computation.3 | async-start | bytes 8650752 | tf_op jit(solution)/shard_map/all_gather | solution.py:13
  10.8 270.1 %copy-start.2 = (f32[128,256]{1,0:T(8,128)S(1)}, f32[128,256]{1,0:T(8,128)}, u32[]{:S(2)}) copy-start(f32[128,256]{1,0:T(8,128)} %param.9) | copy-start | bytes 393220
  10.8 270.1 %copy-start.3 = (f32[128,256]{1,0:T(8,128)S(1)}, f32[128,256]{1,0:T(8,128)}, u32[]{:S(2)}) copy-start(f32[128,256]{1,0:T(8,128)} %param.10) | copy-start | bytes 393220
  15.0 267.6 %all-to-all-start = ((bf16[128,32,256]{0,2,1:T(8,128)(2,1)}), bf16[128,32,256]{0,2,1:T(8,128)(2,1)S(1)}, u32[]{:S(2)}, u32[]{:S(2)}) async-start(bf16[128,32,256]{0,2,1:T(8,128)(2,1)} %bitcast.1), calls=%async_computation | async-start | bytes 4194304 | tf_op jit(solution)/shard_map/all_to_all | solution.py:16
  282.6 1.3 copy-start.1
  283.9 15.2 %copy-start = (bf16[128,8192]{1,0:T(8,128)(2,1)S(1)}, bf16[128,8192]{1,0:T(8,128)(2,1)}, u32[]{:S(2)}) copy-start(bf16[128,8192]{1,0:T(8,128)(2,1)} %param.7) | copy-start | bytes 6291460
Sparse Core Ops, SparseCore 0:
  12.3 268.5 all-reduce.1
Sparse Core Ops, SparseCore 1:
  13.5 154.3 all-gather.3
  171.0 128.0 all-gather.5
where the time goes:
time: 314 us; the launch traced here: 312 us
  waiting for transfers between devices  259 us (82%)
  starting transfers between devices  17.3 us (6%)
  between operations  15.5 us (5%)
  matrix products  11.5 us (4%)
  local copies, waits for them, and re-layouts  5.45 us (2%)
  other arithmetic  3.22 us (1%)
    psum x1, waiting for transfers between devices, body(): pseudo = lax.psum(delta, 'island') / width_island  249 us
    all_to_all x1, starting transfers between devices, body(): lax.all_to_all(layer_input, 'fsdp', split_axis=1, concat_axis=0, tiled=True)  17.2 us
    all_gather x1, waiting for transfers between devices, body(): lax.all_gather(weight, 'fsdp', axis=0, tiled=True)  9 us
  transfers between devices with their start and end apart: 4, of which 2 were waited for; matrix products, arithmetic and copies ran while one was open for 4% of the time, Pallas kernels for 0%

commit v1 on v0

v1 whole, which is shorter than its diff:
```python
import functools

import jax
import jax.numpy as jnp
from jax import lax
from jax.experimental import pallas as pl
from jax.experimental.pallas import tpu as pltpu
from jax.sharding import PartitionSpec as P

MESH = pl.DeviceIdType.MESH
TOK, WIDTH, FEAT, ROWS = 128, 8192, 512, 256
LEFT, RIGHT = 0, 1
FAR, OWN = 0, 1

X0 = 0
DK0 = X0 + 12
WY = DK0 + 6
WC0 = WY + 1
WZ0 = WC0 + 4
GC0 = WZ0 + 2
GZ0 = GC0 + 4
GY = GZ0 + 2
K0 = GY + 1
FX0 = K0 + 6
FZ0 = FX0 + 3
FA0 = FZ0 + 3
FB0 = FA0 + 3
COPIES = FB0 + 3


def dot(a, b):
    return jnp.dot(a, b, preferred_element_type=jnp.float32)


def dot_rows(a, b):
    return lax.dot_general(a, b, (((0,), (0,)), ((), ())), preferred_element_type=jnp.float32)


def kernel(
    dk_ref, x_ref, w_ref, outer_ref, mom_ref, inner_ref,
    keys_ref, grad_ref, new_outer_ref, new_mom_ref,
    xs, dks, ws, part, ksend, krecv, g, gcore, gzs, gzr, gys, gyr,
    fx, acc, fz, pseudo, send, recv, local,
):
    island, f = lax.axis_index("island"), lax.axis_index("fsdp")
    x, zl = island // 4, island % 4
    zh, y, c = f // 16, (f // 2) % 8, f % 2

    def at(dx=0, dzl=0, dzh=0, dy=0, dc=0):
        return (
            ((x + dx) % 4) * 4 + (zl + dzl) % 4,
            ((zh + dzh) % 2) * 16 + ((y + dy + 8) % 8) * 2 + (c + dc) % 2,
        )

    def copy(src, dst, sem, to):
        return pltpu.make_async_remote_copy(
            src_ref=src, dst_ref=dst, send_sem=send.at[sem], recv_sem=recv.at[sem],
            device_id=to, device_id_type=MESH,
        )

    started = []

    def start(src, dst, sem, to):
        moved = copy(src, dst, sem, to)
        moved.start()
        started.append(moved)
        return moved

    def cols(owner, plane):
        return pl.ds(pl.multiple_of(((plane + 2) % 2) * 4096 + ((owner + 8) % 8) * 512, 512), 512)

    def tok(d):
        return pl.ds(d * TOK, TOK)

    mine = pl.ds(pl.multiple_of(c * ROWS, ROWS), ROWS)
    other = pl.ds(pl.multiple_of((1 - c) * ROWS, ROWS), ROWS)
    plane = [zh + 1, zh]

    loads = []
    for role in (LEFT, RIGHT):
        loads.append((dk_ref, dks.at[role, tok(0)]))
        for p in (FAR, OWN):
            loads.append((x_ref.at[:, cols(y - role, plane[p])], xs.at[p, role, tok(0)]))
    loads.append((w_ref.at[0], ws.at[OWN, LEFT, mine]))
    loads = [pltpu.make_async_copy(s, d, local.at[k]) for k, (s, d) in enumerate(loads)]
    for load in loads:
        load.start()

    barrier = pltpu.get_barrier_semaphore()
    partners = [at(dy=d) for d in (1, -1, 2, -2, 3, -3)]
    partners += [at(dc=1), at(dzh=1)]
    partners += [at(dx=k) for k in (1, 2, 3)] + [at(dzl=k) for k in (1, 2, 3)]
    for partner in partners:
        pl.semaphore_signal(barrier, inc=1, device_id=partner, device_id_type=MESH)
    pl.semaphore_wait(barrier, len(partners))

    sign = (1, -1)

    def x_copy(p, role, d):
        owner = y + d if role == LEFT else y - d - 1
        return (
            x_ref.at[:, cols(owner, plane[p])], xs.at[p, role, tok(d)],
            X0 + p * 6 + role * 3 + d - 1, at(dy=sign[role] * d),
        )

    def dk_copy(role, d):
        src = dk_ref if d == 1 else dks.at[role, tok(d - 1)]
        return src, dks.at[role, tok(d)], DK0 + role * 3 + d - 1, at(dy=sign[role])

    def w_core(p, role):
        src = w_ref.at[0] if (p, role) == (OWN, LEFT) else ws.at[p, role, mine]
        return src, ws.at[p, role, mine], WC0 + p * 2 + role, at(dc=1)

    def w_far(role):
        src = w_ref.at[0] if role == LEFT else ws.at[OWN, role, mine]
        return src, ws.at[FAR, role, mine], WZ0 + role, at(dzh=1)

    w_next = (w_ref.at[0], ws.at[OWN, RIGHT, mine], WY, at(dy=1))

    def k_copy(role, d):
        return ksend.at[role, d - 1], krecv.at[role, d - 1], K0 + role * 3 + d - 1, at(dy=-sign[role])

    def arrived(args):
        copy(*args).wait_recv()

    start(*dk_copy(LEFT, 1))
    start(*dk_copy(RIGHT, 1))
    start(*w_next)
    start(*w_far(LEFT))
    start(*w_core(OWN, LEFT))
    for k in (1, 2, 3):
        peer = (x + k) % 4
        start(inner_ref.at[pl.ds(pl.multiple_of(peer * 32, 32), 32)], fx.at[k - 1], FX0 + k - 1, at(dx=k))
    for d in (3, 2, 1):
        for role in (LEFT, RIGHT):
            start(*x_copy(FAR, role, d))

    for role in (LEFT, RIGHT):
        arrived(dk_copy(role, 1))
        start(*dk_copy(role, 2))
    arrived(w_next)
    start(*w_far(RIGHT))
    start(*w_core(OWN, RIGHT))
    for role in (LEFT, RIGHT):
        arrived(dk_copy(role, 2))
        start(*dk_copy(role, 3))
    for d in (3, 2, 1):
        for role in (LEFT, RIGHT):
            start(*x_copy(OWN, role, d))

    block = pl.ds(pl.multiple_of(x * 32, 32), 32)
    eight = pl.ds(pl.multiple_of(x * 32 + zl * 8, 8), 8)
    outer_block = outer_ref[block, :]
    total = outer_block - inner_ref[block, :].astype(jnp.float32)
    for k in (1, 2, 3):
        copy(fx.at[k - 1], fx.at[k - 1], FX0 + k - 1, at(dx=k)).wait_recv()
        total = total + (outer_block - fx[k - 1].astype(jnp.float32))
    acc[...] = total
    for k in (1, 2, 3):
        peer = (zl + k) % 4
        start(acc.at[pl.ds(pl.multiple_of(peer * 8, 8), 8)], fz.at[k - 1], FZ0 + k - 1, at(dzl=k))

    for load in loads:
        load.wait()
    arrived(w_far(LEFT))
    start(*w_core(FAR, LEFT))

    for role in (LEFT, RIGHT):
        for d in (3, 2, 1):
            arrived(x_copy(FAR, role, d))
        arrived(dk_copy(role, 3))
        g[FAR, role] = dot_rows(xs[FAR, role], dks[role])
        start(g.at[FAR, role, other], gcore.at[FAR, role], GC0 + FAR * 2 + role, at(dc=1))

    total = acc[pl.ds(pl.multiple_of(zl * 8, 8), 8), :]
    for k in (1, 2, 3):
        copy(fz.at[k - 1], fz.at[k - 1], FZ0 + k - 1, at(dzl=k)).wait_recv()
        total = total + fz[k - 1]
    pseudo[eight, :] = total / 16
    for k in (1, 2, 3):
        start(pseudo.at[eight], pseudo.at[eight], FA0 + k - 1, at(dzl=k))

    for role in (RIGHT, LEFT):
        copy(gcore.at[FAR, role], gcore.at[FAR, role], GC0 + FAR * 2 + role, at(dc=1)).wait_recv()
        gzs[role] = (g[FAR, role, mine, :] + gcore[FAR, role]).astype(jnp.bfloat16)
        start(gzs.at[role], gzr.at[role], GZ0 + role, at(dzh=1))

    for k in (1, 2, 3):
        came = pl.ds(pl.multiple_of(x * 32 + ((zl + 4 - k) % 4) * 8, 8), 8)
        copy(pseudo.at[came], pseudo.at[came], FA0 + k - 1, at(dzl=k)).wait_recv()
    for k in (1, 2, 3):
        start(pseudo.at[block], pseudo.at[block], FB0 + k - 1, at(dx=k))

    arrived(w_far(RIGHT))
    start(*w_core(FAR, RIGHT))
    for role in (LEFT, RIGHT):
        for p in (FAR, OWN):
            arrived(w_core(p, role))
    for role in (LEFT, RIGHT):
        part[role] = dot(xs[FAR, role], ws[FAR, role])

    for d in (3, 2, 1):
        for role in (LEFT, RIGHT):
            arrived(x_copy(OWN, role, d))
            value = part[role, tok(d), :] + dot(xs[OWN, role, tok(d), :], ws[OWN, role])
            if d < 3:
                arrived(k_copy(role, d + 1))
                value = value + krecv[role, d].astype(jnp.float32)
            ksend[role, d - 1] = value.astype(jnp.bfloat16)
            start(*k_copy(role, d))

    for role in (RIGHT, LEFT):
        g[OWN, role] = dot_rows(xs[OWN, role], dks[role])
        start(g.at[OWN, role, other], gcore.at[OWN, role], GC0 + OWN * 2 + role, at(dc=1))

    def own_total(role):
        copy(gcore.at[OWN, role], gcore.at[OWN, role], GC0 + OWN * 2 + role, at(dc=1)).wait_recv()
        copy(gzs.at[role], gzr.at[role], GZ0 + role, at(dzh=1)).wait_recv()
        return g[OWN, role, mine, :] + gcore[OWN, role] + gzr[role].astype(jnp.float32)

    gys[...] = own_total(RIGHT).astype(jnp.bfloat16)
    start(gys, gyr, GY, at(dy=-1))
    g[OWN, LEFT, mine, :] = own_total(LEFT)

    for k in (1, 2, 3):
        came = pl.ds(pl.multiple_of(((x + 4 - k) % 4) * 32, 32), 32)
        copy(pseudo.at[came], pseudo.at[came], FB0 + k - 1, at(dx=k)).wait_recv()
    new_mom = 0.9 * mom_ref[...] + pseudo[...]
    new_mom_ref[...] = new_mom
    new_outer_ref[...] = outer_ref[...] - 0.7 * (pseudo[...] + 0.9 * new_mom)

    own_keys = part[LEFT, tok(0), :] + part[RIGHT, tok(0), :]
    for role in (LEFT, RIGHT):
        own_keys = own_keys + dot(xs[OWN, role, tok(0), :], ws[OWN, role])
    for role in (LEFT, RIGHT):
        arrived(k_copy(role, 1))
        own_keys = own_keys + krecv[role, 0].astype(jnp.float32)
    keys_ref[...] = own_keys.astype(jnp.bfloat16)

    copy(gys, gyr, GY, at(dy=-1)).wait_recv()
    grad_ref[...] = g[OWN, LEFT, mine, :] + gyr[...].astype(jnp.float32)

    for moved in started:
        moved.wait_send()


def body(key_grad, layer_input, key_weight, outer_frag, momentum, inner_frag):
    whole = pl.BlockSpec(memory_space=pltpu.VMEM)
    bf16, f32 = jnp.bfloat16, jnp.float32
    keys, grad, new_outer, new_momentum = pl.pallas_call(
        kernel,
        name="exchange",
        out_shape=(
            jax.ShapeDtypeStruct((TOK, FEAT), bf16),
            jax.ShapeDtypeStruct((ROWS, FEAT), f32),
            jax.ShapeDtypeStruct(outer_frag.shape, f32),
            jax.ShapeDtypeStruct(outer_frag.shape, f32),
        ),
        in_specs=[pl.BlockSpec(memory_space=pl.ANY)] * 3 + [whole] * 3,
        out_specs=(whole,) * 4,
        scratch_shapes=[
            pltpu.VMEM((2, 2, 4 * TOK, 512), bf16),
            pltpu.VMEM((2, 4 * TOK, FEAT), bf16),
            pltpu.VMEM((2, 2, 2 * ROWS, FEAT), bf16),
            pltpu.VMEM((2, 4 * TOK, FEAT), f32),
            pltpu.VMEM((2, 3, TOK, FEAT), bf16),
            pltpu.VMEM((2, 3, TOK, FEAT), bf16),
            pltpu.VMEM((2, 2, 2 * ROWS, FEAT), f32),
            pltpu.VMEM((2, 2, ROWS, FEAT), f32),
            pltpu.VMEM((2, ROWS, FEAT), bf16),
            pltpu.VMEM((2, ROWS, FEAT), bf16),
            pltpu.VMEM((ROWS, FEAT), bf16),
            pltpu.VMEM((ROWS, FEAT), bf16),
            pltpu.VMEM((3, 32, 256), bf16),
            pltpu.VMEM((32, 256), f32),
            pltpu.VMEM((3, 8, 256), f32),
            pltpu.VMEM((128, 256), f32),
            pltpu.SemaphoreType.DMA((COPIES,)),
            pltpu.SemaphoreType.DMA((COPIES,)),
            pltpu.SemaphoreType.DMA((7,)),
        ],
        compiler_params=pltpu.CompilerParams(
            collective_id=0, has_side_effects=True, vmem_limit_bytes=40 << 20
        ),
    )(key_grad, layer_input, key_weight, outer_frag, momentum, inner_frag)
    return keys, grad[None], new_outer, new_momentum


def solution(mesh):
    placed = (
        P(("island", "fsdp"), None),
        P(("island", "fsdp"), None),
        P("island", "fsdp", None),
        P(None, "fsdp"),
        P(None, "fsdp"),
        P("island", "fsdp"),
    )
    return jax.shard_map(
        body,
        mesh=mesh,
        in_specs=placed,
        out_specs=(
            P(("island", "fsdp"), None),
            P("island", "fsdp", None),
            P(None, "fsdp"),
            P(None, "fsdp"),
        ),
        check_vma=False,
    )
```

time: 314 us -> 100 us (0.32)
  the two profiles are of different devices: /device:TPU:1 before, /device:TPU:504 now
where the time goes in v1:
time: 100 us; the launch traced here: 99.8 us
  Pallas kernels  90.3 us (90%)
  local copies, waits for them, and re-layouts  8.84 us (9%)
    pallas_call x1, Pallas kernels, body(): pl.pallas_call(kernel, name='exchange', out_shape=(jax.ShapeDtypeStruct((...  90.3 us
    unnamed x16, local copies, waits for them, and re-layouts  8.84 us

profile of v1, /device:TPU:504, one launch (start us, length us, event | category | flops | bytes accessed | tf_op | source)
XLA Modules:
  0.0 99.8 jit_solution(7401727112516344220)
XLA Ops:
  0.6 0.0 copy-start
  0.6 1.6 %copy-done = bf16[128,8192]{1,0:T(8,128)(2,1)S(1)} copy-done((bf16[128,8192]{1,0:T(8,128)(2,1)S(1)}, bf16[128,8192]{1,0:T(8,128)(2,1)}, u32[]{:S(2)}) %copy-start) | copy-done | bytes 2097176
  2.2 0.0 copy-start.1
  2.2 0.9 copy-done.1
  3.2 0.0 copy-start.2
  3.2 0.9 copy-done.2
  4.1 0.0 copy-start.3
  4.1 0.9 copy-done.3
  5.0 0.0 copy-start.4
  5.0 0.9 copy-done.4
  5.9 0.0 copy-start.5
  5.9 0.8 copy-done.5
  6.7 90.3 %exchange.1 = (bf16[128,512]{1,0:T(8,128)(2,1)S(1)}, f32[256,512]{1,0:T(8,128)S(1)}, f32[128,256]{1,0:T(8,128)S(1)}, f32[128,256]{1,0:T(8,128)S(1)}) custom-call(bf16[128,512]{1,0:T(8,128)(2,1)S(1)} %copy-done.2, bf16[128,8192]{1,0:T(8,128)(2,1)S(1)} %copy-done, bf16[1,256,512]{2,1,0:T(8,128)(2,1)S(1)} %copy-done.1, f32[128,256]{1,0:T(8,128)S(1)} %copy-done.3, ...), custom_call_target="tpu_custom_call" | custom-call | tf_op jit(solution)/shard_map/exchange/pallas_call | solution.py:250
  97.0 0.7 copy.14
  97.7 0.8 copy.15
  98.5 0.7 copy.16
  99.1 0.7 copy.17
Async XLA Ops:
  0.6 1.6 %copy-start = (bf16[128,8192]{1,0:T(8,128)(2,1)S(1)}, bf16[128,8192]{1,0:T(8,128)(2,1)}, u32[]{:S(2)}) copy-start(bf16[128,8192]{1,0:T(8,128)(2,1)} %x_ref.1) | copy-start | bytes 6291460
  2.2 0.9 copy-start.1
  3.2 0.9 copy-start.2
  4.1 0.9 copy-start.3
  5.0 0.9 copy-start.4
  5.9 0.8 copy-start.5

commit v2 on v1

--- a/solution.py
+++ b/solution.py
@@ -11,6 +11,7 @@
 TOK, WIDTH, FEAT, ROWS = 128, 8192, 512, 256
 LEFT, RIGHT = 0, 1
 FAR, OWN = 0, 1
+VMEM_MB = 56
 
 X0 = 0
 DK0 = X0 + 12
@@ -37,10 +38,10 @@
 
 
 def kernel(
-    dk_ref, x_ref, w_ref, outer_ref, mom_ref, inner_ref,
+    dk_ref, x_ref, w_ref, outer_hbm, mom_hbm, inner_hbm,
     keys_ref, grad_ref, new_outer_ref, new_mom_ref,
     xs, dks, ws, part, ksend, krecv, g, gcore, gzs, gzr, gys, gyr,
-    fx, acc, fz, pseudo, send, recv, local,
+    outer_ref, mom_ref, inner_ref, fx, acc, fz, pseudo, send, recv, local,
 ):
     island, f = lax.axis_index("island"), lax.axis_index("fsdp")
     x, zl = island // 4, island % 4
@@ -82,6 +83,7 @@
         for p in (FAR, OWN):
             loads.append((x_ref.at[:, cols(y - role, plane[p])], xs.at[p, role, tok(0)]))
     loads.append((w_ref.at[0], ws.at[OWN, LEFT, mine]))
+    loads += [(inner_hbm, inner_ref), (outer_hbm, outer_ref), (mom_hbm, mom_ref)]
     loads = [pltpu.make_async_copy(s, d, local.at[k]) for k, (s, d) in enumerate(loads)]
     for load in loads:
         load.start()
@@ -123,131 +125,183 @@
     def arrived(args):
         copy(*args).wait_recv()
 
-    start(*dk_copy(LEFT, 1))
-    start(*dk_copy(RIGHT, 1))
+    order = [(p, d) for p in (FAR, OWN) for d in (3, 2, 1)]
+    under_way, left = ([], []), []
+
+    def send_x(role):
+        sent = under_way[role]
+        if len(sent) >= 3:
+            sent[-3].wait_send()
+            left.append(id(sent[-3]))
+        p, d = order[len(sent)]
+        sent.append(start(*x_copy(p, role, d)))
+
+    both = (RIGHT, LEFT)
+    for role in both:
+        start(*dk_copy(role, 1))
     start(*w_next)
     start(*w_far(LEFT))
     start(*w_core(OWN, LEFT))
     for k in (1, 2, 3):
         peer = (x + k) % 4
-        start(inner_ref.at[pl.ds(pl.multiple_of(peer * 32, 32), 32)], fx.at[k - 1], FX0 + k - 1, at(dx=k))
-    for d in (3, 2, 1):
-        for role in (LEFT, RIGHT):
-            start(*x_copy(FAR, role, d))
-
-    for role in (LEFT, RIGHT):
+        start(inner_hbm.at[pl.ds(pl.multiple_of(peer * 32, 32), 32)], fx.at[k - 1], FX0 + k - 1, at(dx=k))
+    for _ in range(3):
+        for role in both:
+            send_x(role)
+
+    for role in both:
         arrived(dk_copy(role, 1))
         start(*dk_copy(role, 2))
     arrived(w_next)
     start(*w_far(RIGHT))
     start(*w_core(OWN, RIGHT))
-    for role in (LEFT, RIGHT):
+    for role in both:
         arrived(dk_copy(role, 2))
         start(*dk_copy(role, 3))
-    for d in (3, 2, 1):
-        for role in (LEFT, RIGHT):
-            start(*x_copy(OWN, role, d))
+
+    for load in loads:
+        load.wait()
 
     block = pl.ds(pl.multiple_of(x * 32, 32), 32)
     eight = pl.ds(pl.multiple_of(x * 32 + zl * 8, 8), 8)
     outer_block = outer_ref[block, :]
     total = outer_block - inner_ref[block, :].astype(jnp.float32)
     for k in (1, 2, 3):
-        copy(fx.at[k - 1], fx.at[k - 1], FX0 + k - 1, at(dx=k)).wait_recv()
+        arrived((fx.at[k - 1], fx.at[k - 1], FX0 + k - 1, at(dx=k)))
         total = total + (outer_block - fx[k - 1].astype(jnp.float32))
     acc[...] = total
     for k in (1, 2, 3):
         peer = (zl + k) % 4
         start(acc.at[pl.ds(pl.multiple_of(peer * 8, 8), 8)], fz.at[k - 1], FZ0 + k - 1, at(dzl=k))
 
-    for load in loads:
-        load.wait()
+    for role in both:
+        send_x(role)
+
+    total = acc[pl.ds(pl.multiple_of(zl * 8, 8), 8), :]
+    for k in (1, 2, 3):
+        arrived((fz.at[k - 1], fz.at[k - 1], FZ0 + k - 1, at(dzl=k)))
+        total = total + fz[k - 1]
+    pseudo[eight, :] = total / 16
+    for k in (1, 2, 3):
+        start(pseudo.at[eight], pseudo.at[eight], FA0 + k - 1, at(dzl=k))
+
     arrived(w_far(LEFT))
     start(*w_core(FAR, LEFT))
 
-    for role in (LEFT, RIGHT):
+    for role in both:
+        send_x(role)
+
+    def g_core(p, role):
+        return g.at[p, role, other], gcore.at[p, role], GC0 + p * 2 + role, at(dc=1)
+
+    def far_product(role):
         for d in (3, 2, 1):
             arrived(x_copy(FAR, role, d))
         arrived(dk_copy(role, 3))
         g[FAR, role] = dot_rows(xs[FAR, role], dks[role])
-        start(g.at[FAR, role, other], gcore.at[FAR, role], GC0 + FAR * 2 + role, at(dc=1))
-
-    total = acc[pl.ds(pl.multiple_of(zl * 8, 8), 8), :]
-    for k in (1, 2, 3):
-        copy(fz.at[k - 1], fz.at[k - 1], FZ0 + k - 1, at(dzl=k)).wait_recv()
-        total = total + fz[k - 1]
-    pseudo[eight, :] = total / 16
-    for k in (1, 2, 3):
-        start(pseudo.at[eight], pseudo.at[eight], FA0 + k - 1, at(dzl=k))
-
-    for role in (RIGHT, LEFT):
-        copy(gcore.at[FAR, role], gcore.at[FAR, role], GC0 + FAR * 2 + role, at(dc=1)).wait_recv()
+        start(*g_core(FAR, role))
+
+    def far_total(role):
+        arrived(g_core(FAR, role))
         gzs[role] = (g[FAR, role, mine, :] + gcore[FAR, role]).astype(jnp.bfloat16)
         start(gzs.at[role], gzr.at[role], GZ0 + role, at(dzh=1))
 
+    far_product(RIGHT)
+    send_x(RIGHT)
+    far_total(RIGHT)
+    far_product(LEFT)
+    send_x(LEFT)
+    far_total(LEFT)
+
     for k in (1, 2, 3):
         came = pl.ds(pl.multiple_of(x * 32 + ((zl + 4 - k) % 4) * 8, 8), 8)
-        copy(pseudo.at[came], pseudo.at[came], FA0 + k - 1, at(dzl=k)).wait_recv()
+        arrived((pseudo.at[came], pseudo.at[came], FA0 + k - 1, at(dzl=k)))
     for k in (1, 2, 3):
         start(pseudo.at[block], pseudo.at[block], FB0 + k - 1, at(dx=k))
 
     arrived(w_far(RIGHT))
     start(*w_core(FAR, RIGHT))
-    for role in (LEFT, RIGHT):
+    for role in both:
         for p in (FAR, OWN):
             arrived(w_core(p, role))
-    for role in (LEFT, RIGHT):
+    for role in both:
         part[role] = dot(xs[FAR, role], ws[FAR, role])
 
-    for d in (3, 2, 1):
-        for role in (LEFT, RIGHT):
+    def pass_keys(role, d, here=False):
+        if not here:
             arrived(x_copy(OWN, role, d))
-            value = part[role, tok(d), :] + dot(xs[OWN, role, tok(d), :], ws[OWN, role])
-            if d < 3:
-                arrived(k_copy(role, d + 1))
-                value = value + krecv[role, d].astype(jnp.float32)
-            ksend[role, d - 1] = value.astype(jnp.bfloat16)
-            start(*k_copy(role, d))
-
-    for role in (RIGHT, LEFT):
-        g[OWN, role] = dot_rows(xs[OWN, role], dks[role])
-        start(g.at[OWN, role, other], gcore.at[OWN, role], GC0 + OWN * 2 + role, at(dc=1))
+        value = part[role, tok(d), :] + dot(xs[OWN, role, tok(d), :], ws[OWN, role])
+        if d < 3:
+            arrived(k_copy(role, d + 1))
+            value = value + krecv[role, d].astype(jnp.float32)
+        ksend[role, d - 1] = value.astype(jnp.bfloat16)
+        start(*k_copy(role, d))
+
+    soon, late = pl.ds(0, 2 * TOK), pl.ds(2 * TOK, 2 * TOK)
+
+    def own_late(role):
+        g[OWN, role] = dot_rows(xs[OWN, role, late, :], dks[role, late, :])
+
+    def own_soon(role):
+        g[OWN, role] += dot_rows(xs[OWN, role, soon, :], dks[role, soon, :])
+        start(*g_core(OWN, role))
 
     def own_total(role):
-        copy(gcore.at[OWN, role], gcore.at[OWN, role], GC0 + OWN * 2 + role, at(dc=1)).wait_recv()
-        copy(gzs.at[role], gzr.at[role], GZ0 + role, at(dzh=1)).wait_recv()
+        arrived(g_core(OWN, role))
+        arrived((gzs.at[role], gzr.at[role], GZ0 + role, at(dzh=1)))
         return g[OWN, role, mine, :] + gcore[OWN, role] + gzr[role].astype(jnp.float32)
 
+    pass_keys(RIGHT, 3)
+    pass_keys(LEFT, 3)
+    pass_keys(RIGHT, 2)
+    own_late(RIGHT)
+    pass_keys(LEFT, 2)
+    own_late(LEFT)
+    arrived(x_copy(OWN, RIGHT, 1))
+    own_soon(RIGHT)
+    pass_keys(RIGHT, 1, here=True)
     gys[...] = own_total(RIGHT).astype(jnp.bfloat16)
     start(gys, gyr, GY, at(dy=-1))
-    g[OWN, LEFT, mine, :] = own_total(LEFT)
+    pass_keys(LEFT, 1)
+    own_soon(LEFT)
+
+    own_keys = part[LEFT, tok(0), :] + part[RIGHT, tok(0), :]
+    for role in both:
+        own_keys = own_keys + dot(xs[OWN, role, tok(0), :], ws[OWN, role])
+    part[LEFT, tok(0), :] = own_keys
 
     for k in (1, 2, 3):
         came = pl.ds(pl.multiple_of(((x + 4 - k) % 4) * 32, 32), 32)
-        copy(pseudo.at[came], pseudo.at[came], FB0 + k - 1, at(dx=k)).wait_recv()
+        arrived((pseudo.at[came], pseudo.at[came], FB0 + k - 1, at(dx=k)))
     new_mom = 0.9 * mom_ref[...] + pseudo[...]
     new_mom_ref[...] = new_mom
     new_outer_ref[...] = outer_ref[...] - 0.7 * (pseudo[...] + 0.9 * new_mom)
 
-    own_keys = part[LEFT, tok(0), :] + part[RIGHT, tok(0), :]
-    for role in (LEFT, RIGHT):
-        own_keys = own_keys + dot(xs[OWN, role, tok(0), :], ws[OWN, role])
-    for role in (LEFT, RIGHT):
+    g[OWN, LEFT, mine, :] = own_total(LEFT)
+
+    own_keys = part[LEFT, tok(0), :]
+    for role in both:
         arrived(k_copy(role, 1))
         own_keys = own_keys + krecv[role, 0].astype(jnp.float32)
     keys_ref[...] = own_keys.astype(jnp.bfloat16)
 
-    copy(gys, gyr, GY, at(dy=-1)).wait_recv()
+    arrived((gys, gyr, GY, at(dy=-1)))
     grad_ref[...] = g[OWN, LEFT, mine, :] + gyr[...].astype(jnp.float32)
 
     for moved in started:
-        moved.wait_send()
+        if id(moved) not in left:
+            moved.wait_send()
+
+
+def finish(*refs):
+    for k in range(4):
+        refs[4 + k][...] = refs[k][...]
 
 
 def body(key_grad, layer_input, key_weight, outer_frag, momentum, inner_frag):
     whole = pl.BlockSpec(memory_space=pltpu.VMEM)
     bf16, f32 = jnp.bfloat16, jnp.float32
-    keys, grad, new_outer, new_momentum = pl.pallas_call(
+    results = pl.pallas_call(
         kernel,
         name="exchange",
         out_shape=(
@@ -256,7 +310,7 @@
             jax.ShapeDtypeStruct(outer_frag.shape, f32),
             jax.ShapeDtypeStruct(outer_frag.shape, f32),
         ),
-        in_specs=[pl.BlockSpec(memory_space=pl.ANY)] * 3 + [whole] * 3,
+        in_specs=[pl.BlockSpec(memory_space=pltpu.HBM)] * 6,
         out_specs=(whole,) * 4,
         scratch_shapes=[
             pltpu.VMEM((2, 2, 4 * TOK, 512), bf16),
@@ -271,18 +325,28 @@
             pltpu.VMEM((2, ROWS, FEAT), bf16),
             pltpu.VMEM((ROWS, FEAT), bf16),
             pltpu.VMEM((ROWS, FEAT), bf16),
+            pltpu.VMEM((128, 256), f32),
+            pltpu.VMEM((128, 256), f32),
+            pltpu.VMEM((128, 256), bf16),
             pltpu.VMEM((3, 32, 256), bf16),
             pltpu.VMEM((32, 256), f32),
             pltpu.VMEM((3, 8, 256), f32),
             pltpu.VMEM((128, 256), f32),
             pltpu.SemaphoreType.DMA((COPIES,)),
             pltpu.SemaphoreType.DMA((COPIES,)),
-            pltpu.SemaphoreType.DMA((7,)),
+            pltpu.SemaphoreType.DMA((10,)),
         ],
         compiler_params=pltpu.CompilerParams(
-            collective_id=0, has_side_effects=True, vmem_limit_bytes=40 << 20
+            collective_id=0, has_side_effects=True, vmem_limit_bytes=VMEM_MB << 20
         ),
     )(key_grad, layer_input, key_weight, outer_frag, momentum, inner_frag)
+    keys, grad, new_outer, new_momentum = pl.pallas_call(
+        finish,
+        name="finish",
+        out_shape=[jax.ShapeDtypeStruct(r.shape, r.dtype) for r in results],
+        in_specs=[whole] * 4,
+        out_specs=[whole] * 4,
+    )(*results)
     return keys, grad[None], new_outer, new_momentum
 
 

time: 100 us -> 83.7 us (0.84)
  the two profiles are of different devices: /device:TPU:504 before, /device:TPU:1 now
where the time goes in v2:
time: 83.7 us; the launch traced here: 82.7 us
  Pallas kernels  82 us (98%)
    pallas_call x1, Pallas kernels, body(): pl.pallas_call(kernel, name='exchange', out_shape=(jax.ShapeDtypeStruct((...  79.9 us
    pallas_call x1, Pallas kernels, body(): pl.pallas_call(finish, name='finish', out_shape=[jax.ShapeDtypeStruct(r.s...  2.09 us

profile of v2, /device:TPU:1, one launch (start us, length us, event | category | flops | bytes accessed | tf_op | source)
XLA Modules:
  0.0 82.7 jit_solution(5280868070892618056)
XLA Ops:
  0.6 79.9 %exchange.1 = (bf16[128,512]{1,0:T(8,128)(2,1)}, f32[256,512]{1,0:T(8,128)}, f32[128,256]{1,0:T(8,128)}, f32[128,256]{1,0:T(8,128)}) custom-call(bf16[128,512]{1,0:T(8,128)(2,1)} %dk_ref.1, bf16[128,8192]{1,0:T(8,128)(2,1)} %x_ref.1, bf16[1,256,512]{2,1,0:T(8,128)(2,1)} %w_ref.1, f32[128,256]{1,0:T(8,128)} %outer_hbm.1, f32[128,256]{1,0:T(8,128)} %mom_hbm.1, ...), custom_call_target="tpu_custom_call" | custom-call | tf_op jit(solution)/shard_map/exchange/pallas_call | solution.py:304
  80.6 2.1 %finish.1 = (bf16[128,512]{1,0:T(8,128)(2,1)}, f32[256,512]{1,0:T(8,128)}, f32[128,256]{1,0:T(8,128)}, f32[128,256]{1,0:T(8,128)}) custom-call(bf16[128,512]{1,0:T(8,128)(2,1)} %get-tuple-element.12.refs_0_, f32[256,512]{1,0:T(8,128)} %get-tuple-element.13.refs_1_, f32[128,256]{1,0:T(8,128)} %get-tuple-element.14.refs_2_, f32[128,256]{1,0:T(8,128)} %get-tuple-element.15.refs_3_), custom_call_target="tpu_custom_call" | custom-call | tf_op jit(solution)/shard_map/finish/pallas_call | solution.py:343

commit v3 on v2

--- a/solution.py
+++ b/solution.py
@@ -11,10 +11,14 @@
 TOK, WIDTH, FEAT, ROWS = 128, 8192, 512, 256
 LEFT, RIGHT = 0, 1
 FAR, OWN = 0, 1
-VMEM_MB = 56
+VMEM_MB = 40
+FINISH_KB = 53248
+PLAN = ((1, 1, 1, 1, 1, 1, 1, 1, 1, 1), (1, 1, 1, 1, 1, 1, 1, 1, 1, 1))
+DEPTH = (2, 2)
+ORDER = ('a3', 'a2', 'a1', 'o3', 'b3', 'b2', 'b1', 'o2', 'o1')
 
 X0 = 0
-DK0 = X0 + 12
+DK0 = X0 + 18
 WY = DK0 + 6
 WC0 = WY + 1
 WZ0 = WC0 + 4
@@ -41,7 +45,7 @@
     dk_ref, x_ref, w_ref, outer_hbm, mom_hbm, inner_hbm,
     keys_ref, grad_ref, new_outer_ref, new_mom_ref,
     xs, dks, ws, part, ksend, krecv, g, gcore, gzs, gzr, gys, gyr,
-    outer_ref, mom_ref, inner_ref, fx, acc, fz, pseudo, send, recv, local,
+    outer_ref, mom_ref, inner_ref, fx, acc, fz, pseudo, send, recv, local, entered,
 ):
     island, f = lax.axis_index("island"), lax.axis_index("fsdp")
     x, zl = island // 4, island % 4
@@ -67,8 +71,14 @@
         started.append(moved)
         return moved
 
-    def cols(owner, plane):
-        return pl.ds(pl.multiple_of(((plane + 2) % 2) * 4096 + ((owner + 8) % 8) * 512, 512), 512)
+    def cols(owner, plane, h=None):
+        first = ((plane + 2) % 2) * 4096 + ((owner + 8) % 8) * 512
+        if h is None:
+            return pl.ds(pl.multiple_of(first, 512), 512)
+        return pl.ds(pl.multiple_of(first + h * 256, 256), 256)
+
+    def part_cols(h):
+        return pl.ds(0, 512) if h is None else pl.ds(h * 256, 256)
 
     def tok(d):
         return pl.ds(d * TOK, TOK)
@@ -89,20 +99,27 @@
         load.start()
 
     barrier = pltpu.get_barrier_semaphore()
-    partners = [at(dy=d) for d in (1, -1, 2, -2, 3, -3)]
-    partners += [at(dc=1), at(dzh=1)]
-    partners += [at(dx=k) for k in (1, 2, 3)] + [at(dzl=k) for k in (1, 2, 3)]
-    for partner in partners:
-        pl.semaphore_signal(barrier, inc=1, device_id=partner, device_id_type=MESH)
-    pl.semaphore_wait(barrier, len(partners))
+
+    def tell(semaphore, partner):
+        pl.semaphore_signal(semaphore, inc=1, device_id=partner, device_id_type=MESH)
+
+    level = [at(dy=d) for d in (1, -1, 2, -2, 3, -3)] + [at(dc=1)] + [at(dx=k) for k in (1, 2, 3)]
+    upright = [(at(dzh=1), zh == 0)] + [(at(dzl=k), zl + k < 4) for k in (1, 2, 3)]
+    for partner in level:
+        tell(barrier, partner)
+    for partner, is_higher in upright:
+        pl.when(is_higher)(functools.partial(tell, barrier, partner))
+    pl.semaphore_wait(barrier, len(level) + zh + zl)
+    for partner, is_higher in upright:
+        pl.when(jnp.logical_not(is_higher))(functools.partial(tell, entered.at[0 if partner is upright[0][0] else 1], partner))
 
     sign = (1, -1)
 
-    def x_copy(p, role, d):
+    def x_copy(p, role, d, h):
         owner = y + d if role == LEFT else y - d - 1
         return (
-            x_ref.at[:, cols(owner, plane[p])], xs.at[p, role, tok(d)],
-            X0 + p * 6 + role * 3 + d - 1, at(dy=sign[role] * d),
+            x_ref.at[:, cols(owner, plane[p], h)], xs.at[p, role, tok(d), part_cols(h)],
+            X0 + (2 * p + (h or 0)) * 6 + role * 3 + d - 1, at(dy=sign[role] * d),
         )
 
     def dk_copy(role, d):
@@ -122,42 +139,62 @@
     def k_copy(role, d):
         return ksend.at[role, d - 1], krecv.at[role, d - 1], K0 + role * 3 + d - 1, at(dy=-sign[role])
 
+    seen = set()
+
     def arrived(args):
-        copy(*args).wait_recv()
-
-    order = [(p, d) for p in (FAR, OWN) for d in (3, 2, 1)]
+        if args[2] not in seen:
+            seen.add(args[2])
+            copy(*args).wait_recv()
+
+    kinds = {"a": (FAR, 0), "b": (FAR, 1), "o": (OWN, None)}
+    order = [(kinds[e[0]][0], int(e[1]), kinds[e[0]][1]) for e in ORDER]
     under_way, left = ([], []), []
+    both = (RIGHT, LEFT)
 
     def send_x(role):
-        sent = under_way[role]
-        if len(sent) >= 3:
-            sent[-3].wait_send()
-            left.append(id(sent[-3]))
-        p, d = order[len(sent)]
-        sent.append(start(*x_copy(p, role, d)))
-
-    both = (RIGHT, LEFT)
+        sent, depth = under_way[role], DEPTH[role]
+        if len(sent) == len(order):
+            return
+        if len(sent) >= depth:
+            sent[-depth].wait_send()
+            left.append(id(sent[-depth]))
+        p, d, h = order[len(sent)]
+        sent.append(start(*x_copy(p, role, d, h)))
+
+    def send_both(site):
+        for role in both:
+            for _ in range(PLAN[role][site]):
+                send_x(role)
+
     for role in both:
         start(*dk_copy(role, 1))
     start(*w_next)
-    start(*w_far(LEFT))
+    first_far = copy(*w_far(LEFT))
+    started.append(first_far)
+    pl.when(zh == 1)(first_far.start)
     start(*w_core(OWN, LEFT))
     for k in (1, 2, 3):
         peer = (x + k) % 4
         start(inner_hbm.at[pl.ds(pl.multiple_of(peer * 32, 32), 32)], fx.at[k - 1], FX0 + k - 1, at(dx=k))
-    for _ in range(3):
-        for role in both:
-            send_x(role)
+    send_both(0)
 
     for role in both:
         arrived(dk_copy(role, 1))
         start(*dk_copy(role, 2))
+    send_both(1)
+
+    @pl.when(zh == 0)
+    def _():
+        pl.semaphore_wait(entered.at[0], 1)
+        first_far.start()
+
     arrived(w_next)
     start(*w_far(RIGHT))
     start(*w_core(OWN, RIGHT))
     for role in both:
         arrived(dk_copy(role, 2))
         start(*dk_copy(role, 3))
+    send_both(2)
 
     for load in loads:
         load.wait()
@@ -170,12 +207,16 @@
         arrived((fx.at[k - 1], fx.at[k - 1], FX0 + k - 1, at(dx=k)))
         total = total + (outer_block - fx[k - 1].astype(jnp.float32))
     acc[...] = total
+
+    @pl.when(zl < 3)
+    def _():
+        pl.semaphore_wait(entered.at[1], 3 - zl)
+
     for k in (1, 2, 3):
         peer = (zl + k) % 4
         start(acc.at[pl.ds(pl.multiple_of(peer * 8, 8), 8)], fz.at[k - 1], FZ0 + k - 1, at(dzl=k))
 
-    for role in both:
-        send_x(role)
+    send_both(3)
 
     total = acc[pl.ds(pl.multiple_of(zl * 8, 8), 8), :]
     for k in (1, 2, 3):
@@ -188,58 +229,77 @@
     arrived(w_far(LEFT))
     start(*w_core(FAR, LEFT))
 
-    for role in both:
-        send_x(role)
+    send_both(4)
 
     def g_core(p, role):
         return g.at[p, role, other], gcore.at[p, role], GC0 + p * 2 + role, at(dc=1)
 
-    def far_product(role):
+    def far_product(role, h):
         for d in (3, 2, 1):
-            arrived(x_copy(FAR, role, d))
-        arrived(dk_copy(role, 3))
-        g[FAR, role] = dot_rows(xs[FAR, role], dks[role])
-        start(*g_core(FAR, role))
-
-    def far_total(role):
-        arrived(g_core(FAR, role))
-        gzs[role] = (g[FAR, role, mine, :] + gcore[FAR, role]).astype(jnp.bfloat16)
-        start(gzs.at[role], gzr.at[role], GZ0 + role, at(dzh=1))
-
-    far_product(RIGHT)
-    send_x(RIGHT)
-    far_total(RIGHT)
-    far_product(LEFT)
-    send_x(LEFT)
-    far_total(LEFT)
+            arrived(x_copy(FAR, role, d, h))
+        if h == 0:
+            arrived(dk_copy(role, 3))
+        g[FAR, role, pl.ds(h * 256, 256), :] = dot_rows(xs[FAR, role, :, part_cols(h)], dks[role])
+        moved = copy(*g_core(FAR, role))
+        pl.when(c != h)(moved.start)
+
+    def far_total(role, h):
+        came = copy(*g_core(FAR, role))
+        moved = copy(gzs.at[role], gzr.at[role], GZ0 + role, at(dzh=1))
+
+        @pl.when(c == h)
+        def _():
+            came.wait_recv()
+            gzs[role] = (g[FAR, role, pl.ds(h * 256, 256), :] + gcore[FAR, role]).astype(jnp.bfloat16)
+            moved.start()
+
+    for role in both:
+        far_product(role, 0)
+    for role in both:
+        far_total(role, 0)
+    send_both(5)
 
     for k in (1, 2, 3):
         came = pl.ds(pl.multiple_of(x * 32 + ((zl + 4 - k) % 4) * 8, 8), 8)
         arrived((pseudo.at[came], pseudo.at[came], FA0 + k - 1, at(dzl=k)))
     for k in (1, 2, 3):
         start(pseudo.at[block], pseudo.at[block], FB0 + k - 1, at(dx=k))
-
     arrived(w_far(RIGHT))
     start(*w_core(FAR, RIGHT))
+
+    send_both(6)
     for role in both:
         for p in (FAR, OWN):
             arrived(w_core(p, role))
-    for role in both:
-        part[role] = dot(xs[FAR, role], ws[FAR, role])
-
-    def pass_keys(role, d, here=False):
-        if not here:
-            arrived(x_copy(OWN, role, d))
-        value = part[role, tok(d), :] + dot(xs[OWN, role, tok(d), :], ws[OWN, role])
+
+    def keys_part(role, d):
+        return dot(xs[FAR, role, tok(d), :], ws[FAR, role]) + dot(xs[OWN, role, tok(d), :], ws[OWN, role])
+
+    def pass_keys(role, d):
+        arrived(x_copy(FAR, role, d, 0))
+        arrived(x_copy(FAR, role, d, 1))
+        arrived(x_copy(OWN, role, d, None))
+        value = keys_part(role, d)
         if d < 3:
             arrived(k_copy(role, d + 1))
             value = value + krecv[role, d].astype(jnp.float32)
         ksend[role, d - 1] = value.astype(jnp.bfloat16)
         start(*k_copy(role, d))
 
+    for role in both:
+        pass_keys(role, 3)
+    send_both(7)
+    for role in both:
+        far_product(role, 1)
+    for role in both:
+        far_total(role, 1)
+    send_both(8)
+
     soon, late = pl.ds(0, 2 * TOK), pl.ds(2 * TOK, 2 * TOK)
 
     def own_late(role):
+        arrived(x_copy(OWN, role, 3, None))
+        arrived(x_copy(OWN, role, 2, None))
         g[OWN, role] = dot_rows(xs[OWN, role, late, :], dks[role, late, :])
 
     def own_soon(role):
@@ -251,24 +311,20 @@
         arrived((gzs.at[role], gzr.at[role], GZ0 + role, at(dzh=1)))
         return g[OWN, role, mine, :] + gcore[OWN, role] + gzr[role].astype(jnp.float32)
 
-    pass_keys(RIGHT, 3)
-    pass_keys(LEFT, 3)
+    own_keys = keys_part(LEFT, 0) + keys_part(RIGHT, 0)
+    part[...] = own_keys
+    pass_keys(LEFT, 2)
+    own_late(RIGHT)
+    send_both(9)
+    arrived(x_copy(OWN, RIGHT, 1, None))
+    own_soon(RIGHT)
     pass_keys(RIGHT, 2)
-    own_late(RIGHT)
-    pass_keys(LEFT, 2)
     own_late(LEFT)
-    arrived(x_copy(OWN, RIGHT, 1))
-    own_soon(RIGHT)
-    pass_keys(RIGHT, 1, here=True)
     gys[...] = own_total(RIGHT).astype(jnp.bfloat16)
     start(gys, gyr, GY, at(dy=-1))
+    pass_keys(RIGHT, 1)
     pass_keys(LEFT, 1)
     own_soon(LEFT)
-
-    own_keys = part[LEFT, tok(0), :] + part[RIGHT, tok(0), :]
-    for role in both:
-        own_keys = own_keys + dot(xs[OWN, role, tok(0), :], ws[OWN, role])
-    part[LEFT, tok(0), :] = own_keys
 
     for k in (1, 2, 3):
         came = pl.ds(pl.multiple_of(((x + 4 - k) % 4) * 32, 32), 32)
@@ -279,7 +335,7 @@
 
     g[OWN, LEFT, mine, :] = own_total(LEFT)
 
-    own_keys = part[LEFT, tok(0), :]
+    own_keys = part[...]
     for role in both:
         arrived(k_copy(role, 1))
         own_keys = own_keys + krecv[role, 0].astype(jnp.float32)
@@ -288,17 +344,25 @@
     arrived((gys, gyr, GY, at(dy=-1)))
     grad_ref[...] = g[OWN, LEFT, mine, :] + gyr[...].astype(jnp.float32)
 
+    for role in both:
+        copy(*g_core(FAR, role)).wait_send()
+        copy(gzs.at[role], gzr.at[role], GZ0 + role, at(dzh=1)).wait_send()
     for moved in started:
         if id(moved) not in left:
             moved.wait_send()
 
 
 def finish(*refs):
-    for k in range(4):
-        refs[4 + k][...] = refs[k][...]
+    moves = [pltpu.make_async_copy(refs[k], refs[4 + k], refs[8].at[k]) for k in range(4)]
+    for move in moves:
+        move.start()
+    for move in moves:
+        move.wait()
 
 
 def body(key_grad, layer_input, key_weight, outer_frag, momentum, inner_frag):
+    held = (key_grad, layer_input, key_weight, outer_frag, momentum, inner_frag)
+    held = [pltpu.with_memory_space_constraint(a, pltpu.HBM) for a in held]
     whole = pl.BlockSpec(memory_space=pltpu.VMEM)
     bf16, f32 = jnp.bfloat16, jnp.float32
     results = pl.pallas_call(
@@ -310,13 +374,13 @@
             jax.ShapeDtypeStruct(outer_frag.shape, f32),
             jax.ShapeDtypeStruct(outer_frag.shape, f32),
         ),
-        in_specs=[pl.BlockSpec(memory_space=pltpu.HBM)] * 6,
+        in_specs=[pl.BlockSpec(memory_space=pl.ANY)] * 6,
         out_specs=(whole,) * 4,
         scratch_shapes=[
             pltpu.VMEM((2, 2, 4 * TOK, 512), bf16),
             pltpu.VMEM((2, 4 * TOK, FEAT), bf16),
             pltpu.VMEM((2, 2, 2 * ROWS, FEAT), bf16),
-            pltpu.VMEM((2, 4 * TOK, FEAT), f32),
+            pltpu.VMEM((TOK, FEAT), f32),
             pltpu.VMEM((2, 3, TOK, FEAT), bf16),
             pltpu.VMEM((2, 3, TOK, FEAT), bf16),
             pltpu.VMEM((2, 2, 2 * ROWS, FEAT), f32),
@@ -335,17 +399,20 @@
             pltpu.SemaphoreType.DMA((COPIES,)),
             pltpu.SemaphoreType.DMA((COPIES,)),
             pltpu.SemaphoreType.DMA((10,)),
+            pltpu.SemaphoreType.REGULAR((2,)),
         ],
         compiler_params=pltpu.CompilerParams(
             collective_id=0, has_side_effects=True, vmem_limit_bytes=VMEM_MB << 20
         ),
-    )(key_grad, layer_input, key_weight, outer_frag, momentum, inner_frag)
+    )(*held)
     keys, grad, new_outer, new_momentum = pl.pallas_call(
         finish,
         name="finish",
         out_shape=[jax.ShapeDtypeStruct(r.shape, r.dtype) for r in results],
         in_specs=[whole] * 4,
-        out_specs=[whole] * 4,
+        out_specs=[pl.BlockSpec(memory_space=pl.ANY)] * 4,
+        scratch_shapes=[pltpu.SemaphoreType.DMA((4,))],
+        compiler_params=pltpu.CompilerParams(vmem_limit_bytes=FINISH_KB << 10),
     )(*results)
     return keys, grad[None], new_outer, new_momentum
 

time: 83.7 us -> 76.9 us (0.919)
  Pallas kernels: 82 us -> 76 us
    pallas_call x1, Pallas kernels: 79.9 us -> 75.1 us  [body(): pl.pallas_call(kernel, name='exchange', out_shape=(jax.ShapeDtypeStruct((...]
    pallas_call x1, Pallas kernels: 2.09 us -> 0.95 us  [body(): pl.pallas_call(finish, name='finish', out_shape=[jax.ShapeDtypeStruct(r.s...]
where the time goes in v3:
time: 76.9 us; the launch traced here: 76.7 us
  Pallas kernels  76 us (99%)
    pallas_call x1, Pallas kernels, body(): pl.pallas_call(kernel, name='exchange', out_shape=(jax.ShapeDtypeStruct((...  75.1 us

profile of v3, /device:TPU:1, one launch (start us, length us, event | category | flops | bytes accessed | tf_op | source)
XLA Modules:
  0.0 76.7 jit_solution(13083845031321330758)
XLA Ops:
  0.6 75.1 %exchange.1 = (bf16[128,512]{1,0:T(8,128)(2,1)S(1)}, f32[256,512]{1,0:T(8,128)S(1)}, f32[128,256]{1,0:T(8,128)S(1)}, f32[128,256]{1,0:T(8,128)S(1)}) custom-call(bf16[128,512]{1,0:T(8,128)(2,1)} %dk_ref.1, bf16[128,8192]{1,0:T(8,128)(2,1)} %x_ref.1, bf16[1,256,512]{2,1,0:T(8,128)(2,1)} %w_ref.1, f32[128,256]{1,0:T(8,128)} %outer_hbm.1, f32[128,256]{1,0:T(8,128)} %mom_hbm.1, ...), custom_call_target="tpu_custom_call" | custom-call | tf_op jit(solution)/shard_map/exchange/pallas_call | solution.py:368
  75.7 1.0 %finish.1 = (bf16[128,512]{1,0:T(8,128)(2,1)}, f32[256,512]{1,0:T(8,128)}, f32[128,256]{1,0:T(8,128)}, f32[128,256]{1,0:T(8,128)}) custom-call(bf16[128,512]{1,0:T(8,128)(2,1)S(1)} %get-tuple-element.12.refs_0_, f32[256,512]{1,0:T(8,128)S(1)} %get-tuple-element.13.refs_1_, f32[128,256]{1,0:T(8,128)S(1)} %get-tuple-element.14.refs_2_, ...), custom_call_target="tpu_custom_call" | custom-call | tf_op jit(solution)/shard_map/finish/pallas_call | solution.py:408

commit v4 on v3

--- a/solution.py
+++ b/solution.py
@@ -311,20 +311,20 @@
         arrived((gzs.at[role], gzr.at[role], GZ0 + role, at(dzh=1)))
         return g[OWN, role, mine, :] + gcore[OWN, role] + gzr[role].astype(jnp.float32)
 
+    pass_keys(LEFT, 2)
+    pass_keys(RIGHT, 2)
     own_keys = keys_part(LEFT, 0) + keys_part(RIGHT, 0)
     part[...] = own_keys
-    pass_keys(LEFT, 2)
     own_late(RIGHT)
     send_both(9)
     arrived(x_copy(OWN, RIGHT, 1, None))
     own_soon(RIGHT)
-    pass_keys(RIGHT, 2)
     own_late(LEFT)
     gys[...] = own_total(RIGHT).astype(jnp.bfloat16)
     start(gys, gyr, GY, at(dy=-1))
-    pass_keys(RIGHT, 1)
     pass_keys(LEFT, 1)
     own_soon(LEFT)
+    pass_keys(RIGHT, 1)
 
     for k in (1, 2, 3):
         came = pl.ds(pl.multiple_of(((x + 4 - k) % 4) * 32, 32), 32)

time: 76.9 us -> 76.1 us (0.990)
  no operation moved by 1% of the time
where the time goes in v4:
time: 76.1 us; the launch traced here: 76 us
  Pallas kernels  75.3 us (99%)
    pallas_call x1, Pallas kernels, body(): pl.pallas_call(kernel, name='exchange', out_shape=(jax.ShapeDtypeStruct((...  74.4 us

profile of v4, /device:TPU:1, one launch (start us, length us, event | category | flops | bytes accessed | tf_op | source)
XLA Modules:
  0.0 76.0 jit_solution(16187597881490428754)
XLA Ops:
  0.6 74.4 %exchange.1 = (bf16[128,512]{1,0:T(8,128)(2,1)S(1)}, f32[256,512]{1,0:T(8,128)S(1)}, f32[128,256]{1,0:T(8,128)S(1)}, f32[128,256]{1,0:T(8,128)S(1)}) custom-call(bf16[128,512]{1,0:T(8,128)(2,1)} %dk_ref.1, bf16[128,8192]{1,0:T(8,128)(2,1)} %x_ref.1, bf16[1,256,512]{2,1,0:T(8,128)(2,1)} %w_ref.1, f32[128,256]{1,0:T(8,128)} %outer_hbm.1, f32[128,256]{1,0:T(8,128)} %mom_hbm.1, ...), custom_call_target="tpu_custom_call" | custom-call | tf_op jit(solution)/shard_map/exchange/pallas_call | solution.py:368
  75.0 1.0 %finish.1 = (bf16[128,512]{1,0:T(8,128)(2,1)}, f32[256,512]{1,0:T(8,128)}, f32[128,256]{1,0:T(8,128)}, f32[128,256]{1,0:T(8,128)}) custom-call(bf16[128,512]{1,0:T(8,128)(2,1)S(1)} %get-tuple-element.12.refs_0_, f32[256,512]{1,0:T(8,128)S(1)} %get-tuple-element.13.refs_1_, f32[128,256]{1,0:T(8,128)S(1)} %get-tuple-element.14.refs_2_, ...), custom_call_target="tpu_custom_call" | custom-call | tf_op jit(solution)/shard_map/finish/pallas_call | solution.py:408
